TPU v7x, 32 devices: a whole 2x2x4 slice. The times are simulated.
32 devices in a mesh: tm: 8 (over z, x), space: 4 (over y, core).
Axes of the slice: x: 2, y: 2, z: 4, core: 2. Of those that a mesh axis runs over, the one named last changes fastest.
Arguments:
- queries: bfloat16 [8, 2560, 2240], P('tm', 'space'), may hold values from -6 to 6
- keys: bfloat16 [8, 2560, 2240], P('tm', 'space'), may hold values from -6 to 6
- values: bfloat16 [8, 2560, 2240], P('tm', 'space'), may hold values from -6 to 6
- gain: float32 [2240], replicated, may hold values from 0.1 to 1.9
- out_weight: bfloat16 [2240, 2240], P('tm'), may hold values from -0.125 to 0.125
Outputs:
- projected: bfloat16 [8, 2560, 2240], P('tm', 'space')
All inputs are finite; a program needn't handle non-finite values.
Results may differ from a plain program's by a relative error of at most 0.0075.
Values may be sent and summed in bfloat16 or wider, within the bound.
A program may use at most 128 MiB of HBM per device.

v0:
```python
import jax
import jax.numpy as jnp
from jax import lax
from jax.sharding import PartitionSpec as P

HEADS = 20
HEAD_DIM = 112


def prefix_2(value, axis, join, neutral):
    place = lax.axis_index(axis)
    gathered = jax.tree.map(
        lambda a, kind: lax.all_gather(a.astype(kind), axis), value, (jnp.bfloat16, jnp.bfloat16)
    )
    state = jax.tree.map(lambda a, e: jnp.zeros_like(a) + jnp.asarray(e, a.dtype), value, neutral)

    def one(lap, state):
        return join(
            state,
            jax.tree.map(
                lambda a, own: lax.dynamic_index_in_dim(a, lap, 0, False).astype(own.dtype),
                gathered,
                value,
            ),
        )

    return lax.fori_loop(0, place, one, state)


def add_pair(earlier, later):
    return (earlier[0] + later[0], earlier[1] + later[1])


def local(queries, keys, values, gain, out_weight):
    rows = queries.shape[1]
    width = queries.shape[2]
    flat_size = HEADS * HEAD_DIM * HEAD_DIM
    fk = jnp.maximum(keys[0], 0).reshape(rows, HEADS, HEAD_DIM)
    vals = values[0].reshape(rows, HEADS, HEAD_DIM)
    state = jnp.einsum("shi,shj->hij", fk, vals, preferred_element_type=jnp.float32).reshape(
        flat_size
    )
    norm_part = jnp.sum(fk.astype(jnp.float32), axis=0).reshape(HEADS * HEAD_DIM)
    share, share_norm = (
        lax.psum_scatter(state, "space", scatter_dimension=0, tiled=True),
        lax.psum_scatter(norm_part, "space", scatter_dimension=0, tiled=True),
    )
    earlier, earlier_norm = prefix_2(
        (share, share_norm), "tm", add_pair, (jnp.zeros_like(share), jnp.zeros_like(share_norm))
    )
    total, total_norm = (
        lax.all_gather(earlier + share, "space", axis=0, tiled=True),
        lax.all_gather(earlier_norm + share_norm, "space", axis=0, tiled=True),
    )
    prefix = total.reshape(HEADS, HEAD_DIM, HEAD_DIM)
    prefix_norm = total_norm.reshape(HEADS, HEAD_DIM)
    fq = jnp.maximum(queries[0], 0).astype(jnp.float32).reshape(rows, HEADS, HEAD_DIM)
    numer = jnp.einsum("shi,hij->shj", fq, prefix, precision=lax.Precision.HIGHEST)
    denom = jnp.einsum("shi,hi->sh", fq, prefix_norm, precision=lax.Precision.HIGHEST) + 1.0
    mixed = (numer / denom[:, :, None]).reshape(rows, width)
    meansq = jnp.mean(mixed * mixed, axis=-1, keepdims=True)
    normed = (mixed * lax.rsqrt(meansq + 1e-06) * gain).astype(jnp.bfloat16)
    result = jnp.dot(
        normed,
        lax.all_gather(out_weight, "tm", axis=0, tiled=True),
        preferred_element_type=jnp.float32,
    )
    result = result.astype(jnp.bfloat16)
    return result[None]


def solution(mesh):
    return jax.shard_map(
        local,
        mesh=mesh,
        in_specs=(
            P("tm", "space", None),
            P("tm", "space", None),
            P("tm", "space", None),
            P(),
            P("tm", None),
        ),
        out_specs=P("tm", "space", None),
        check_vma=False,
    )
```

profile of v0, /device:TPU:0, one launch (start us, length us, event | category | flops | bytes accessed | tf_op | source)
XLA Modules:
  0.0 220.2 jit_solution(13916275081430820619)
XLA Ops:
  7.4 2.2 %broadcast_maximum_fusion.1 = bf16[1,640,2240]{1,2,0:T(8,128)(2,1)S(1)} fusion(bf16[1,640,2240]{1,2,0:T(8,128)(2,1)} %param.8), kind=kLoop, calls=%fused_computation.11 | loop fusion | flops 1433600 | bytes 5734400 | tf_op jit(solution)/shard_map/max | solution.py:38
  9.6 0.5 copy-done
  10.0 2.1 fusion.5
  12.1 3.1 %reshape.37 = f32[250880]{0:T(1024)} reshape(f32[20,112,112]{2,1,0:T(8,128)} %fusion.5) | data formatting | bytes 2007040 | tf_op jit(solution)/shard_map/reshape | solution.py:40
  15.3 0.0 all-gather.6.cloned.1.call-start
  15.3 0.5 all-gather.6.cloned.1.call-update
  15.9 0.6 dynamic-slice
  16.4 0.7 fusion.4
  17.7 2.4 %convert_reduce_fusion.2 = f32[2240]{0:T(1024)S(1)} fusion(bf16[1,640,2240]{1,2,0:T(8,128)(2,1)} %param.8), kind=kLoop, calls=%fused_computation.7 | loop fusion | flops 4298560 | bytes 2876160 | tf_op jit(solution)/shard_map/reduce_sum | solution.py:43
  20.2 13.4 %all-reduce.3 = f32[2240]{0:T(1024)S(1)} all-reduce(f32[2240]{0:T(1024)S(1)} %convert_reduce_fusion.2), channel_id=5, replica_groups=mesh['tm'=8,'space'=4] {'space'}, use_global_device_ids=true, to_apply=%region_2.0.clone | all-reduce | flops 2240 | bytes 17920
  33.6 0.1 dynamic-slice.11
  34.3 0.2 dynamic-update-slice
  34.5 38.3 %all-reduce = bf16[4480]{0:T(1024)(128)(2,1)S(1)} all-reduce(bf16[4480]{0:T(1024)(128)(2,1)S(1)} %dynamic-update-slice), channel_id=3, replica_groups=mesh['tm'=8,'space'=4] {'tm'}, use_global_device_ids=true, to_apply=%add | all-reduce | flops 4480 | bytes 17920
  72.8 0.1 reshape.44
  74.2 3.6 %broadcast_maximum_fusion = bf16[1,640,2240]{1,2,0:T(8,128)(2,1)} fusion(bf16[1,640,2240]{1,2,0:T(8,128)(2,1)} %param.7), kind=kLoop, calls=%fused_computation.10 | loop fusion | flops 1433600 | bytes 5734400 | tf_op jit(solution)/shard_map/max | solution.py:57
  77.9 1.1 dynamic-slice.10
  78.9 0.1 reshape.51
  79.1 53.9 %all-gather.2 = bf16[8,1,62720]{2,1,0:T(2,128)(2,1)S(1)} all-gather(bf16[1,1,62720]{2,1,0:T(2,128)(2,1)S(1)} %reshape.51), channel_id=2, replica_groups=mesh['tm'=8,'space'=4] {'tm'}, dimensions={0}, use_global_device_ids=true | all-gather | bytes 1128960 | tf_op jit(solution)/shard_map/all_gather | solution.py:13
  132.9 1.1 copy.15
  134.1 0.2 add_dynamic-update-slice_fusion
  134.3 10.9 %all-reduce.1 = f32[2240]{0:T(1024)S(1)} all-reduce(f32[2240]{0:T(1024)S(1)} %add_dynamic-update-slice_fusion), channel_id=1, replica_groups=mesh['tm'=8,'space'=4] {'space'}, use_global_device_ids=true, to_apply=%add.1 | all-reduce | flops 2240 | bytes 17920
  145.2 0.1 reshape.64
  145.3 1.1 dynamic-slice_add_fusion
  146.4 0.2 reshape.53
  146.6 9.1 %all-gather.3 = f32[4,1,62720]{2,1,0:T(1,128)} all-gather(f32[1,1,62720]{2,1,0:T(1,128)S(1)} %reshape.53), channel_id=1, replica_groups=mesh['tm'=8,'space'=4] {'space'}, dimensions={0}, use_global_device_ids=true | all-gather | bytes 1254400 | tf_op jit(solution)/shard_map/all_gather | solution.py:52
  155.7 4.8 %reduce.4 = f32[4,62720]{1,0:T(4,128)} reduce(f32[4,1,62720]{2,1,0:T(1,128)} %all-gather.3, f32[]{:T(128)} %constant.58), dimensions={1}, to_apply=%all-gather.3.reduce_sub_computation | reduce | bytes 2007044 | tf_op jit(solution)/shard_map/all_gather | solution.py:52
  160.5 3.4 %reshape.38 = f32[20,112,112]{2,1,0:T(8,128)} reshape(f32[4,62720]{1,0:T(4,128)} %reduce.4) | data formatting | bytes 2007040 | tf_op jit(solution)/shard_map/reshape | solution.py:55
  163.9 3.4 %fusion.6 = f32[20,1,640]{2,1,0:T(1,128)S(1)} fusion(f32[20,112,1]{1,2,0:T(1,128)S(1)} %reshape.64, bf16[640,20,112]{0,2,1:T(8,128)(2,1)} %bitcast.34), kind=kOutput, calls=%fused_computation.22 | convolution fusion | flops 17203200 | bytes 2927360 | tf_op jit(solution)/shard_map/shi,hi->sh/dot_general | solution.py:59
  167.3 4.5 %multiply_reduce_fusion = (f32[640]{0:T(1024)S(1)}, f32[640,20,112]{0,2,1:T(8,128)S(1)}) fusion(f32[640,20]{0,1:T(8,128)S(1)} %fusion.3, f32[20,112,112]{2,1,0:T(8,128)} %reshape.38, bf16[640,20,112]{0,2,1:T(8,128)(2,1)S(1)} %bitcast.35), kind=kOutput, calls=%fused_computation.6 | convolution fusion | flops 1931058560 | bytes 9658880 | tf_op jit(solution)/shard_map/shi,hij->shj/dot_general | solution.py:58
  171.8 2.2 fusion.1
  174.0 25.7 %all-gather.6.cloned.1.call-done = bf16[2240,2240]{1,0:T(8,128)(2,1)} async-done(((bf16[280,2240]{1,0:T(8,128)(2,1)}), bf16[2240,2240]{1,0:T(8,128)(2,1)}) %all-gather.6.cloned.1.call-update) | async-done | bytes 10035216 | tf_op jit(solution)/shard_map/all_gather | solution.py:65
  199.6 13.1 %fusion.2 = bf16[1,640,2240]{1,2,0:T(8,128)(2,1)} fusion(bf16[640,2240]{0,1:T(8,128)(2,1)} %fusion.1, bf16[2240,2240]{1,0:T(8,128)(2,1)} %all-gather.6.cloned.1.call-done), kind=kOutput, calls=%fused_computation.9 | convolution fusion | flops 6423961600 | bytes 15769600 | tf_op jit(solution)/shard_map/dot_general | solution.py:63
  (19 shorter events, 0.1 us)
Async XLA Ops:
  7.4 2.7 %copy-start = (bf16[1,640,2240]{1,2,0:T(8,128)(2,1)S(1)}, bf16[1,640,2240]{1,2,0:T(8,128)(2,1)}, u32[]{:S(2)}) copy-start(bf16[1,640,2240]{1,2,0:T(8,128)(2,1)} %param.9) | copy-start | bytes 8601604
  7.4 70.5 %all-reduce.6.cloned.1.call-start = ((), (), s32[]{:S(2)}) async-start(), calls=%async_computation.1 | async-start | bytes 2007040
  12.1 3.8 %copy-start.4 = (u32[32]{0:T(128)S(1)}, u32[32]{0:T(128)}, u32[]{:S(2)}) copy-start(u32[32]{0:T(128)} %constant.38) | copy-start | bytes 388
  12.1 4.3 %copy-start.3 = (u32[32]{0:T(128)S(1)}, u32[32]{0:T(128)}, u32[]{:S(2)}) copy-start(u32[32]{0:T(128)} %constant.43) | copy-start | bytes 388
  15.3 184.4 %all-gather.6.cloned.1.call-start = ((), (), s32[]{:S(2)}) async-start(), calls=%async_computation | async-start | bytes 11612160 | tf_op jit(solution)/shard_map/all_gather | solution.py:65
  163.9 3.4 %copy-start.1 = (bf16[1,640,2240]{1,2,0:T(8,128)(2,1)S(1)}, bf16[1,640,2240]{1,2,0:T(8,128)(2,1)}, u32[]{:S(2)}) copy-start(bf16[1,640,2240]{1,2,0:T(8,128)(2,1)} %broadcast_maximum_fusion) | copy-start | bytes 8601604
  167.3 4.5 %copy-start.2 = (f32[2240]{0:T(1024)S(1)}, f32[2240]{0:T(1024)}, u32[]{:S(2)}) copy-start(f32[2240]{0:T(1024)} %param.10) | copy-start | bytes 26884
Sparse Core Ops, SparseCore 0:
  15.4 38.8 all-reduce.5
Sparse Core Ops, SparseCore 1:
  18.1 181.4 all-gather.5
where the time goes:
time: 221 us; the launch traced here: 220 us
  blocking collectives  126 us (57%)
  waiting for transfers between devices  26.2 us (12%)
  matrix products  23.1 us (10%)
  between operations  17.5 us (8%)
  other arithmetic  16.5 us (7%)
  local copies, waits for them, and re-layouts  11.2 us (5%)
    unnamed x3, blocking collectives  62.7 us
    all_gather x1, blocking collectives, prefix_2(): lax.all_gather(a.astype(kind), axis)  53.9 us
    all_gather x1, waiting for transfers between devices, local(): lax.all_gather(out_weight, 'tm', axis=0, tiled=True)  25.7 us
    dot_general x1, matrix products, local(): jnp.dot(normed, lax.all_gather(out_weight, 'tm', axis=0, tiled=True), pre...  13.1 us
    all_gather x1, blocking collectives, local(): lax.all_gather(earlier + share, 'space', axis=0, tiled=True)  9.11 us
    all_gather x1, other arithmetic, local(): lax.all_gather(earlier + share, 'space', axis=0, tiled=True)  4.78 us
    unnamed x20, local copies, waits for them, and re-layouts  4.49 us
    dot_general x1, matrix products, local(): jnp.einsum('shi,hij->shj', fq, prefix, precision=lax.Precision.HIGHEST)  4.47 us
  transfers between devices with their start and end apart: 2, of which 1 were waited for; matrix products, arithmetic and copies ran while one was open for 14% of the time, Pallas kernels for 0%

commit v1 on v0

v1 whole, which is shorter than its diff:
```python
import functools

import jax
import jax.numpy as jnp
from jax import lax
from jax.experimental import pallas as pl
from jax.experimental.pallas import tpu as pltpu
from jax.sharding import PartitionSpec as P

HEADS = 20
LANES = 128
MESH = pl.DeviceIdType.MESH


def heads_of(tile, width, dim):
    first = tile * LANES
    last = min(first + LANES, width) - 1
    return range(first // dim, last // dim + 1)


def window(tile, width):
    return max(0, (tile - 1) * LANES), min(width, (tile + 2) * LANES)


def head_lanes(tile, dim):
    column = tile * LANES + lax.broadcasted_iota(jnp.int32, (dim, LANES), 1)
    return column // dim


def state_kernel(dim, k_ref, v_ref, out_ref):
    rows, width = k_ref.shape
    tiles = -(-width // LANES)
    spare = width - (tiles - 1) * LANES
    lane = lax.broadcasted_iota(jnp.int32, (dim, LANES), 1)
    ones = jnp.ones((rows, LANES), jnp.bfloat16)
    norms = jnp.zeros((dim, LANES), jnp.float32)
    done = set()
    for t in range(tiles):
        lo, hi = window(t, width)
        fk = jnp.maximum(k_ref[:, lo:hi], 0)
        end = min((t + 1) * LANES, width)
        v = v_ref[:, t * LANES : end]
        if end - t * LANES < LANES:
            v = jnp.concatenate(
                [v, jnp.zeros((rows, (t + 1) * LANES - end), v.dtype)], axis=1
            )
        both = lax.dot_general(
            fk,
            jnp.concatenate([v, ones], axis=1),
            (((0,), (0,)), ((), ())),
            preferred_element_type=jnp.float32,
        )
        owner = head_lanes(t, dim)
        compact = jnp.zeros((dim, LANES), jnp.float32)
        for h in heads_of(t, width, dim):
            at = h * dim - lo
            compact = jnp.where(owner == h, both[at : at + dim, :LANES], compact)
            if h not in done:
                done.add(h)
                norms = jnp.where(lane == spare + h, both[at : at + dim, LANES:], norms)
        if t == tiles - 1:
            compact = jnp.where(lane >= spare, norms, compact)
        out_ref[t] = compact.astype(out_ref.dtype)
    for t in range(tiles, out_ref.shape[0]):
        out_ref[t] = jnp.zeros((dim, LANES), out_ref.dtype)


def exchange_kernel(
    n, space, part_ref, w_ref, state_ref, wg_ref,
    landed, totals, arrived,
    local_sem, rs_send, rs_recv, scan_send, scan_recv, ag_send, ag_recv,
    tm_send, tm_recv, y_send, y_recv, core_send, core_recv,
):
    t = lax.axis_index("tm")
    s = lax.axis_index("space")
    cores = 2
    ys = space // cores
    y, c = s // cores, s % cores
    bits = []
    d = 1
    while d < n:
        bits.append(d)
        d *= 2

    def flip(m):
        where = t
        for d in bits:
            if m & d:
                where = where + d - 2 * d * ((t // d) % 2)
        return where

    def peer(r):
        return (t, lax.rem(s + r, space))

    barrier = pltpu.get_barrier_semaphore()
    for r in range(1, space):
        pl.semaphore_signal(barrier, inc=1, device_id=peer(r), device_id_type=MESH)
    for d in bits:
        pl.semaphore_signal(barrier, inc=1, device_id=(flip(d), s), device_id_type=MESH)
    pl.semaphore_wait(barrier, space - 1 + len(bits))

    sent = []

    def remote(src, dst, send, recv, device):
        return pltpu.make_async_remote_copy(
            src_ref=src, dst_ref=dst, send_sem=send, recv_sem=recv,
            device_id=device, device_id_type=MESH,
        )

    def go(copy):
        copy.start()
        sent.append(copy)

    for r in range(1, space):
        go(remote(part_ref.at[lax.rem(s + r, space)], landed.at[r],
                  rs_send.at[r], rs_recv.at[r], peer(r)))

    groups = (s, space + c)

    def weight_hop(i, m, d):
        g = groups[i]
        src = w_ref.at[g] if m == 0 else wg_ref.at[g, flip(m)]
        return remote(src, wg_ref.at[g, flip(m)], tm_send.at[i, m + d],
                      tm_recv.at[i, m + d], (flip(d), s))

    def await_weight(i, m):
        low = m & -m
        shard = wg_ref.at[groups[i], flip(m)]
        remote(shard, shard, tm_send.at[i, m], tm_recv.at[i, m], (flip(low), s)).wait_recv()

    def to_core(i, g, m):
        shard = wg_ref.at[g, flip(m)]
        return remote(shard, shard, core_send.at[i, m], core_recv.at[i, m],
                      (t, y * cores + (1 - c)))

    def to_y(r, m):
        shard = wg_ref.at[s, flip(m)]
        return remote(shard, shard, y_send.at[r, m], y_recv.at[r, m],
                      (t, lax.rem(y + r, ys) * cores + c))

    def from_y(r):
        return lax.rem(y + ys - r, ys) * cores + c

    for d in reversed(bits):
        for i in range(2):
            go(weight_hop(i, 0, d))
    own = pltpu.make_async_copy(w_ref, wg_ref.at[:, t], local_sem)
    own.start()

    pending = []

    def pass_on(m):
        for i in range(2):
            await_weight(i, m)
            for d in reversed(bits):
                if d < (m & -m):
                    go(weight_hop(i, m, d))
            if i == 0:
                for r in range(1, ys):
                    go(to_y(r, m))
            go(to_core(i, groups[i], m))
        pending.append(m)

    def settle(m):
        for r in range(1, ys):
            shard = wg_ref.at[from_y(r), flip(m)]
            remote(shard, shard, y_send.at[r, m], y_recv.at[r, m],
                   (t, lax.rem(y + ys - r, ys) * cores + c)).wait_recv()
            go(to_core(1 + r, from_y(r), m))

    order = sorted(range(1, n), key=lambda m: (bin(m).count("1"), -m))
    order = list(order)

    def next_weight():
        if order:
            pass_on(order.pop(0))

    total = part_ref[s].astype(jnp.float32)
    for r in range(1, space):
        remote(part_ref.at[0], landed.at[r], rs_send.at[r], rs_recv.at[r], peer(r)).wait_recv()
        total = total + landed[r].astype(jnp.float32)
    prefix = total
    for k, d in enumerate(bits):
        totals[k] = total.astype(totals.dtype)
        hop = remote(totals.at[k], arrived.at[k], scan_send.at[k], scan_recv.at[k], (flip(d), s))
        go(hop)
        next_weight()
        hop.wait_recv()
        got = arrived[k].astype(jnp.float32)
        prefix = prefix + got * ((t // d) % 2).astype(jnp.float32)
        total = total + got
    state_ref[s] = prefix.astype(state_ref.dtype)
    for r in range(1, space):
        go(remote(state_ref.at[s], state_ref.at[s], ag_send.at[r], ag_recv.at[r], peer(r)))
    while order:
        next_weight()
        if len(pending) > 1:
            settle(pending.pop(0))
    while pending:
        settle(pending.pop(0))
    for r in range(1, space):
        slot = state_ref.at[lax.rem(s + space - r, space)]
        remote(slot, slot, ag_send.at[r], ag_recv.at[r], peer(r)).wait_recv()
    other = 1 - c
    for m in range(1, n):
        sources = [y * cores + other, space + other]
        sources += [lax.rem(y + ys - r, ys) * cores + other for r in range(1, ys)]
        for i, g in enumerate(sources):
            shard = wg_ref.at[g, flip(m)]
            remote(shard, shard, core_send.at[i, m], core_recv.at[i, m],
                   (t, y * cores + other)).wait_recv()
    own.wait()
    for copy in sent:
        copy.wait_send()


def read_kernel(dim, q_ref, state_ref, gain_ref, w_ref, out_ref, mixed, normed):
    rows, width = q_ref.shape
    tiles = -(-width // LANES)
    spare = width - (tiles - 1) * LANES

    @pl.when(pl.program_id(0) == 0)
    def _():
        lane = lax.broadcasted_iota(jnp.int32, (dim, LANES), 1)
        norms = state_ref[tiles - 1].astype(jnp.float32)
        squares = jnp.zeros((rows, LANES), jnp.float32)
        for t in range(tiles):
            lo, hi = window(t, width)
            owner = head_lanes(t, dim)
            part = state_ref[t].astype(jnp.float32)
            rows_of = []
            at = lo
            for h in heads_of(t, width, dim):
                if h * dim > at:
                    rows_of.append(jnp.zeros((h * dim - at, 2 * LANES), jnp.bfloat16))
                norm = jnp.sum(jnp.where(lane == spare + h, norms, 0), axis=1, keepdims=True)
                mine = owner == h
                rows_of.append(
                    jnp.concatenate(
                        [jnp.where(mine, part, 0), jnp.where(mine, norm, 0)], axis=1
                    ).astype(jnp.bfloat16)
                )
                at = (h + 1) * dim
            if at < hi:
                rows_of.append(jnp.zeros((hi - at, 2 * LANES), jnp.bfloat16))
            fq = jnp.maximum(q_ref[:, lo:hi], 0)
            both = jnp.dot(
                fq, jnp.concatenate(rows_of, axis=0), preferred_element_type=jnp.float32
            )
            tile = both[:, :LANES] / (both[:, LANES:] + 1.0)
            mixed[:, t * LANES : (t + 1) * LANES] = tile
            squares = squares + tile * tile
        meansq = jnp.sum(squares, axis=1, keepdims=True) / width
        scale = lax.rsqrt(meansq + 1e-06)
        for t in range(tiles):
            end = min((t + 1) * LANES, width)
            normed[:, t * LANES : end] = (
                mixed[:, t * LANES : end] * scale * gain_ref[:, t * LANES : end]
            ).astype(normed.dtype)

    out_ref[...] = jnp.dot(
        normed[...], w_ref[0], preferred_element_type=jnp.float32
    ).astype(out_ref.dtype)


def local(n, space, queries, keys, values, gain, out_weight):
    _, rows, width = queries.shape
    dim = width // HEADS
    tiles = -(-width // LANES)
    share = -(-tiles // space)
    shard, columns = out_weight.shape
    groups = space + 2
    gw = -(-columns // (groups * LANES)) * LANES
    vmem = pl.BlockSpec(memory_space=pltpu.VMEM)
    big = pltpu.CompilerParams(vmem_limit_bytes=56 * 1024 * 1024)

    w = jnp.pad(out_weight, ((0, 0), (0, groups * gw - columns)))
    w = w.reshape(shard, groups, gw).transpose(1, 0, 2)

    state = pl.pallas_call(
        functools.partial(state_kernel, dim),
        out_shape=jax.ShapeDtypeStruct((space * share, dim, LANES), jnp.bfloat16),
        in_specs=[vmem, vmem],
        out_specs=vmem,
        compiler_params=big,
        name="block_state",
    )(keys[0], values[0])

    steps = n.bit_length() - 1
    dma = pltpu.SemaphoreType.DMA
    piece = (share, dim, LANES)
    prefix, wg = pl.pallas_call(
        functools.partial(exchange_kernel, n, space),
        out_shape=(
            jax.ShapeDtypeStruct((space,) + piece, jnp.bfloat16),
            jax.ShapeDtypeStruct((groups, n, shard, gw), jnp.bfloat16),
        ),
        in_specs=[vmem, pl.BlockSpec(memory_space=pl.ANY)],
        out_specs=(vmem, pl.BlockSpec(memory_space=pl.ANY)),
        scratch_shapes=[
            pltpu.VMEM((space,) + piece, jnp.bfloat16),
            pltpu.VMEM((steps,) + piece, jnp.bfloat16),
            pltpu.VMEM((steps,) + piece, jnp.bfloat16),
            dma,
            dma((space,)), dma((space,)),
            dma((steps,)), dma((steps,)),
            dma((space,)), dma((space,)),
            dma((2, n)), dma((2, n)),
            dma((space // 2, n)), dma((space // 2, n)),
            dma((space // 2 + 1, n)), dma((space // 2 + 1, n)),
        ],
        compiler_params=pltpu.CompilerParams(
            collective_id=0, has_side_effects=True, vmem_limit_bytes=56 * 1024 * 1024
        ),
        name="exchange",
    )(state.reshape((space,) + piece), w)

    out = pl.pallas_call(
        functools.partial(read_kernel, dim),
        grid=(-(-columns // gw),),
        out_shape=jax.ShapeDtypeStruct((rows, columns), jnp.bfloat16),
        in_specs=[
            pl.BlockSpec((rows, width), lambda i: (0, 0)),
            pl.BlockSpec((space * share, dim, LANES), lambda i: (0, 0, 0)),
            pl.BlockSpec((1, width), lambda i: (0, 0)),
            pl.BlockSpec((1, n * shard, gw), lambda i: (i, 0, 0)),
        ],
        out_specs=pl.BlockSpec((rows, gw), lambda i: (0, i)),
        scratch_shapes=[
            pltpu.VMEM((rows, tiles * LANES), jnp.float32),
            pltpu.VMEM((rows, width), jnp.bfloat16),
        ],
        compiler_params=big,
        name="read_project",
    )(
        queries[0],
        prefix.reshape(space * share, dim, LANES),
        gain.reshape(1, width),
        wg.reshape(groups, n * shard, gw),
    )
    return out[None]


def solution(mesh):
    sizes = dict(mesh.shape)
    return jax.shard_map(
        functools.partial(local, sizes["tm"], sizes["space"]),
        mesh=mesh,
        in_specs=(
            P("tm", "space", None),
            P("tm", "space", None),
            P("tm", "space", None),
            P(),
            P("tm", None),
        ),
        out_specs=P("tm", "space", None),
        check_vma=False,
    )
```

time: 221 us -> 122 us (0.55)
  blocking collectives: 126 us -> 0 us
  Pallas kernels: 0 us -> 100 us
  waiting for transfers between devices: 26.2 us -> 0 us
  matrix products: 23.1 us -> 0 us
  between operations: 17.5 us -> 0.02 us
  other arithmetic: 16.5 us -> 0 us
  local copies, waits for them, and re-layouts: 11.2 us -> 22 us
    pallas_call x0 -> x3, Pallas kernels: none -> 100 us  [the longest x1 76.2 us: local(): pl.pallas_call(functools.partial(exchange_kernel, n, space), out_shape=(j...]
    all_gather x2 -> x0, blocking collectives: 63 us -> none  [the longest x1 53.9 us: prefix_2(): lax.all_gather(a.astype(kind), axis)]
    unnamed x3 -> x0, blocking collectives: 62.7 us -> none
    all_gather x1 -> x0, waiting for transfers between devices: 25.7 us -> none  [local(): lax.all_gather(out_weight, 'tm', axis=0, tiled=True)]
    dot_general x4 -> x0, matrix products: 23.1 us -> none  [the longest x1 13.1 us: local(): jnp.dot(normed, lax.all_gather(out_weight, 'tm', axis=0, tiled=True), pre...]
    unnamed x20 -> x7, local copies, waits for them, and re-layouts: 4.49 us -> 12.6 us
    max x2 -> x0, other arithmetic: 5.84 us -> none  [the longest x1 3.63 us: local(): jnp.maximum(queries[0], 0).astype(jnp.float32)]
    broadcast_in_dim x2 -> x1, local copies, waits for them, and re-layouts: 0.02 us -> 5.37 us  [local(): return out[None]]
  transfers between devices with their start and end apart: 2 -> 0, of which waited for: 1 -> 0; matrix products, arithmetic and copies ran while one was open for 14% -> 0% of each run, Pallas kernels for 0% -> 0%
where the time goes in v1:
time: 122 us
  Pallas kernels  100 us (82%)
  local copies, waits for them, and re-layouts  22 us (18%)
    pallas_call x1, Pallas kernels, local(): pl.pallas_call(functools.partial(exchange_kernel, n, space), out_shape=(j...  76.2 us
    pallas_call x1, Pallas kernels, local(): pl.pallas_call(functools.partial(read_kernel, dim), grid=(-(-columns // g...  17.4 us
    unnamed x7, local copies, waits for them, and re-layouts  12.6 us
    pallas_call x1, Pallas kernels, local(): pl.pallas_call(functools.partial(state_kernel, dim), out_shape=jax.ShapeD...  6.38 us
    broadcast_in_dim x1, local copies, waits for them, and re-layouts, local(): return out[None]  5.37 us

profile of v1, /device:TPU:0, one launch (start us, length us, event | category | flops | bytes accessed | tf_op | source)
XLA Modules:
  0.0 122.0 jit_solution(3020621230239037424)
XLA Ops:
  0.0 0.0 copy-start
  0.0 1.5 %reshape.18.gain_ref = f32[1,2240]{1,0:T(1,128)} reshape(f32[2240]{0:T(1024)} %param.8) | data formatting | bytes 17920 | tf_op jit(solution)/shard_map/reshape | solution.py:338
  1.5 1.4 %pad.4 = bf16[280,2304]{1,0:T(8,128)(2,1)S(1)} pad(bf16[280,2240]{1,0:T(8,128)(2,1)} %param.9, bf16[]{:T(256)} %constant.2.clone.1), padding=0_0x0_64 | pad | bytes 2544642 | tf_op jit(solution)/shard_map/jit(_pad)/pad | solution.py:277
  2.9 1.2 copy.17
  4.0 0.0 copy-done
  4.1 3.5 %copy.10 = bf16[1,640,2240]{2,1,0:T(8,128)(2,1)} copy(bf16[1,640,2240]{1,2,0:T(8,128)(2,1)S(1)} %copy-done) | data formatting | bytes 5734400 | tf_op args[0]
  7.6 0.0 copy-start.1
  7.6 5.5 %copy.11 = bf16[1,640,2240]{2,1,0:T(8,128)(2,1)} copy(bf16[1,640,2240]{1,2,0:T(8,128)(2,1)} %param.6) | data formatting | bytes 5734400 | tf_op args[1]
  13.1 0.0 copy-done.1
  13.1 3.5 %copy.12 = bf16[1,640,2240]{2,1,0:T(8,128)(2,1)} copy(bf16[1,640,2240]{1,2,0:T(8,128)(2,1)S(1)} %copy-done.1) | data formatting | bytes 5734400 | tf_op args[2]
  16.6 6.4 %block_state.1 = bf16[20,112,128]{2,1,0:T(8,128)(2,1)} custom-call(bf16[640,2240]{1,0:T(8,128)(2,1)} %bitcast.16, bf16[640,2240]{1,0:T(8,128)(2,1)} %bitcast.17), custom_call_target="tpu_custom_call" | custom-call | tf_op jit(solution)/shard_map/block_state/pallas_call | solution.py:280
  23.0 76.2 %exchange.1 = (bf16[4,5,112,128]{3,2,1,0:T(8,128)(2,1)}, bf16[6,8,280,384]{3,2,1,0:T(8,128)(2,1)}) custom-call(bf16[4,5,112,128]{3,2,1,0:T(8,128)(2,1)} %bitcast.21, bf16[6,280,384]{2,1,0:T(8,128)(2,1)} %bitcast.19), custom_call_target="tpu_custom_call" | custom-call | tf_op jit(solution)/shard_map/exchange/pallas_call | solution.py:292
  99.2 17.4 %read_project.1 = bf16[640,2240]{1,0:T(8,128)(2,1)} custom-call(bf16[640,2240]{1,0:T(8,128)(2,1)} %bitcast.14, bf16[20,112,128]{2,1,0:T(8,128)(2,1)} %bitcast.22, f32[1,2240]{1,0:T(1,128)} %reshape.18.gain_ref, bf16[6,2240,384]{2,1,0:T(8,128)(2,1)} %bitcast.18), custom_call_target="tpu_custom_call" | custom-call | tf_op jit(solution)/shard_map/read_project/pallas_call | solution.py:318
  116.6 5.4 %copy.14 = bf16[1,640,2240]{1,2,0:T(8,128)(2,1)} copy(bf16[1,640,2240]{2,1,0:T(8,128)(2,1)} %bitcast.15) | data formatting | bytes 5734400 | tf_op jit(solution)/shard_map/broadcast_in_dim | solution.py:341
Async XLA Ops:
  0.0 4.1 %copy-start = (bf16[1,640,2240]{1,2,0:T(8,128)(2,1)S(1)}, bf16[1,640,2240]{1,2,0:T(8,128)(2,1)}, u32[]{:S(2)}) copy-start(bf16[1,640,2240]{1,2,0:T(8,128)(2,1)} %param.5) | copy-start | bytes 8601604
  7.6 5.5 %copy-start.1 = (bf16[1,640,2240]{1,2,0:T(8,128)(2,1)S(1)}, bf16[1,640,2240]{1,2,0:T(8,128)(2,1)}, u32[]{:S(2)}) copy-start(bf16[1,640,2240]{1,2,0:T(8,128)(2,1)} %param.7) | copy-start | bytes 8601604

commit v2 on v1

v2 whole, which is shorter than its diff:
```python
import functools

import jax
import jax.numpy as jnp
from jax import lax
from jax.experimental import pallas as pl
from jax.experimental.pallas import tpu as pltpu
from jax.sharding import PartitionSpec as P

HEADS = 20
LANES = 128
MESH = pl.DeviceIdType.MESH


def exchange_kernel(
    n, space, k_ref, v_ref, w_ref, state_ref, wg_ref,
    keys, vals, ones, part_ref, landed, totals, arrived,
    local_sem, load_sem, rs_send, rs_recv, scan_send, scan_recv, ag_send, ag_recv,
    tm_send, tm_recv, y_send, y_recv, core_send, core_recv,
):
    t = lax.axis_index("tm")
    s = lax.axis_index("space")
    cores = 2
    ys = space // cores
    y, c = s // cores, s % cores
    bits = []
    d = 1
    while d < n:
        bits.append(d)
        d *= 2

    def flip(m):
        where = t
        for d in bits:
            if m & d:
                where = where + d - 2 * d * ((t // d) % 2)
        return where

    def peer(r):
        return (t, lax.rem(s + r, space))

    loads = [
        pltpu.make_async_copy(k_ref, keys, load_sem.at[0]),
        pltpu.make_async_copy(v_ref, vals, load_sem.at[1]),
    ]
    for load in loads:
        load.start()

    barrier = pltpu.get_barrier_semaphore()
    for r in range(1, space):
        pl.semaphore_signal(barrier, inc=1, device_id=peer(r), device_id_type=MESH)
    for d in bits:
        pl.semaphore_signal(barrier, inc=1, device_id=(flip(d), s), device_id_type=MESH)
    pl.semaphore_wait(barrier, space - 1 + len(bits))

    sent = []

    def remote(src, dst, send, recv, device):
        return pltpu.make_async_remote_copy(
            src_ref=src, dst_ref=dst, send_sem=send, recv_sem=recv,
            device_id=device, device_id_type=MESH,
        )

    def go(copy):
        copy.start()
        sent.append(copy)

    groups = (s, space + c)

    def weight_hop(i, m, d):
        g = groups[i]
        src = w_ref.at[g] if m == 0 else wg_ref.at[g, flip(m)]
        return remote(src, wg_ref.at[g, flip(m)], tm_send.at[i, m + d],
                      tm_recv.at[i, m + d], (flip(d), s))

    def await_weight(i, m):
        low = m & -m
        shard = wg_ref.at[groups[i], flip(m)]
        remote(shard, shard, tm_send.at[i, m], tm_recv.at[i, m], (flip(low), s)).wait_recv()

    def to_core(i, g, m):
        shard = wg_ref.at[g, flip(m)]
        return remote(shard, shard, core_send.at[i, m], core_recv.at[i, m],
                      (t, y * cores + (1 - c)))

    def to_y(r, m):
        shard = wg_ref.at[s, flip(m)]
        return remote(shard, shard, y_send.at[r, m], y_recv.at[r, m],
                      (t, lax.rem(y + r, ys) * cores + c))

    def from_y(r):
        return lax.rem(y + ys - r, ys) * cores + c

    for d in reversed(bits):
        for i in range(2):
            go(weight_hop(i, 0, d))
    own = pltpu.make_async_copy(w_ref, wg_ref.at[:, t], local_sem)
    own.start()

    heads, dim, _ = keys.shape
    ones[...] = jnp.ones_like(ones)
    for load in loads:
        load.wait()
    share = part_ref.shape[1]

    def one_state(h):
        v = jnp.concatenate([vals[h], ones[...]], axis=0)
        fk = jnp.maximum(keys[h], 0)
        return lax.dot_general(
            v, fk, (((1,), (1,)), ((), ())), preferred_element_type=jnp.float32
        ).astype(part_ref.dtype)

    for h in range(space * share):
        part_ref[h // share, h % share] = (
            one_state(h) if h < heads else jnp.zeros(part_ref.shape[2:], part_ref.dtype)
        )

    for r in range(1, space):
        go(remote(part_ref.at[lax.rem(s + r, space)], landed.at[r],
                  rs_send.at[r], rs_recv.at[r], peer(r)))

    pending = []

    def pass_on(m):
        for i in range(2):
            await_weight(i, m)
            for d in reversed(bits):
                if d < (m & -m):
                    go(weight_hop(i, m, d))
            if i == 0:
                for r in range(1, ys):
                    go(to_y(r, m))
            go(to_core(i, groups[i], m))
        pending.append(m)

    def settle(m):
        for r in range(1, ys):
            shard = wg_ref.at[from_y(r), flip(m)]
            remote(shard, shard, y_send.at[r, m], y_recv.at[r, m],
                   (t, lax.rem(y + ys - r, ys) * cores + c)).wait_recv()
            go(to_core(1 + r, from_y(r), m))

    order = sorted(range(1, n), key=lambda m: (bin(m).count("1"), -m))
    order = list(order)

    def next_weight():
        if order:
            pass_on(order.pop(0))

    total = part_ref[s].astype(jnp.float32)
    for r in range(1, space):
        remote(part_ref.at[0], landed.at[r], rs_send.at[r], rs_recv.at[r], peer(r)).wait_recv()
        total = total + landed[r].astype(jnp.float32)
    prefix = total
    for k, d in enumerate(bits):
        totals[k] = total.astype(totals.dtype)
        hop = remote(totals.at[k], arrived.at[k], scan_send.at[k], scan_recv.at[k], (flip(d), s))
        go(hop)
        next_weight()
        hop.wait_recv()
        got = arrived[k].astype(jnp.float32)
        prefix = prefix + got * ((t // d) % 2).astype(jnp.float32)
        total = total + got
    state_ref[s] = prefix.astype(state_ref.dtype)
    for r in range(1, space):
        go(remote(state_ref.at[s], state_ref.at[s], ag_send.at[r], ag_recv.at[r], peer(r)))
    while order:
        next_weight()
        if len(pending) > 1:
            settle(pending.pop(0))
    while pending:
        settle(pending.pop(0))
    for r in range(1, space):
        slot = state_ref.at[lax.rem(s + space - r, space)]
        remote(slot, slot, ag_send.at[r], ag_recv.at[r], peer(r)).wait_recv()
    other = 1 - c
    for m in range(1, n):
        sources = [y * cores + other, space + other]
        sources += [lax.rem(y + ys - r, ys) * cores + other for r in range(1, ys)]
        for i, g in enumerate(sources):
            shard = wg_ref.at[g, flip(m)]
            remote(shard, shard, core_send.at[i, m], core_recv.at[i, m],
                   (t, y * cores + other)).wait_recv()
    own.wait()
    for copy in sent:
        copy.wait_send()


def read_kernel(q_ref, state_ref, gain_ref, w_ref, out_ref, mixed, normed):
    heads, dim, rows = q_ref.shape

    @pl.when(pl.program_id(0) == 0)
    def _():
        squares = jnp.zeros((1, rows), jnp.float32)
        for h in range(heads):
            both = jnp.dot(
                state_ref[h], jnp.maximum(q_ref[h], 0), preferred_element_type=jnp.float32
            )
            tile = both[:dim] / (both[dim : dim + 1] + 1.0)
            mixed[h] = tile
            squares = squares + jnp.sum(tile * tile, axis=0, keepdims=True)
        scale = lax.rsqrt(squares / (heads * dim) + 1e-06)
        for h in range(heads):
            mixed[h] = mixed[h] * scale * gain_ref[h]
        flat = mixed[...].reshape(heads * dim, rows).astype(normed.dtype)
        normed[...] = flat.T

    out_ref[...] = (
        jnp.dot(normed[...], w_ref[0], preferred_element_type=jnp.float32)
        .astype(out_ref.dtype)
        .T
    )


def local(n, space, queries, keys, values, gain, out_weight):
    _, rows, width = queries.shape
    dim = width // HEADS
    extra = 16
    share = -(-HEADS // space)
    shard, columns = out_weight.shape
    groups = space + 2
    gw = -(-columns // (groups * LANES)) * LANES
    vmem = pl.BlockSpec(memory_space=pltpu.VMEM)
    big = pltpu.CompilerParams(vmem_limit_bytes=56 * 1024 * 1024)

    w = jnp.pad(out_weight, ((0, 0), (0, groups * gw - columns)))
    w = w.reshape(shard, groups, gw).transpose(1, 0, 2)

    def by_head(a):
        return a[0].T.reshape(HEADS, dim, rows)

    steps = n.bit_length() - 1
    dma = pltpu.SemaphoreType.DMA
    piece = (share, dim + extra, dim)
    prefix, wg = pl.pallas_call(
        functools.partial(exchange_kernel, n, space),
        out_shape=(
            jax.ShapeDtypeStruct((space,) + piece, jnp.bfloat16),
            jax.ShapeDtypeStruct((groups, n, shard, gw), jnp.bfloat16),
        ),
        in_specs=[pl.BlockSpec(memory_space=pl.ANY)] * 3,
        out_specs=(vmem, pl.BlockSpec(memory_space=pl.ANY)),
        scratch_shapes=[
            pltpu.VMEM((HEADS, dim, rows), jnp.bfloat16),
            pltpu.VMEM((HEADS, dim, rows), jnp.bfloat16),
            pltpu.VMEM((extra, rows), jnp.bfloat16),
            pltpu.VMEM((space,) + piece, jnp.bfloat16),
            pltpu.VMEM((space,) + piece, jnp.bfloat16),
            pltpu.VMEM((steps,) + piece, jnp.bfloat16),
            pltpu.VMEM((steps,) + piece, jnp.bfloat16),
            dma,
            dma((2,)),
            dma((space,)), dma((space,)),
            dma((steps,)), dma((steps,)),
            dma((space,)), dma((space,)),
            dma((2, n)), dma((2, n)),
            dma((space // 2, n)), dma((space // 2, n)),
            dma((space // 2 + 1, n)), dma((space // 2 + 1, n)),
        ],
        compiler_params=pltpu.CompilerParams(
            collective_id=0, has_side_effects=True, vmem_limit_bytes=56 * 1024 * 1024
        ),
        name="exchange",
    )(by_head(keys), by_head(values), w)

    out = pl.pallas_call(
        read_kernel,
        grid=(-(-columns // gw),),
        out_shape=jax.ShapeDtypeStruct((columns, rows), jnp.bfloat16),
        in_specs=[
            pl.BlockSpec((HEADS, dim, rows), lambda i: (0, 0, 0)),
            pl.BlockSpec((space * share, dim + extra, dim), lambda i: (0, 0, 0)),
            pl.BlockSpec((HEADS, dim, 1), lambda i: (0, 0, 0)),
            pl.BlockSpec((1, n * shard, gw), lambda i: (i, 0, 0)),
        ],
        out_specs=pl.BlockSpec((gw, rows), lambda i: (i, 0)),
        scratch_shapes=[
            pltpu.VMEM((HEADS, dim, rows), jnp.float32),
            pltpu.VMEM((rows, width), jnp.bfloat16),
        ],
        compiler_params=big,
        name="read_project",
    )(
        by_head(queries),
        prefix.reshape((space * share,) + piece[1:]),
        gain.reshape(HEADS, dim, 1),
        wg.reshape(groups, n * shard, gw),
    )
    return out.T[None]


def solution(mesh):
    sizes = dict(mesh.shape)
    return jax.shard_map(
        functools.partial(local, sizes["tm"], sizes["space"]),
        mesh=mesh,
        in_specs=(
            P("tm", "space", None),
            P("tm", "space", None),
            P("tm", "space", None),
            P(),
            P("tm", None),
        ),
        out_specs=P("tm", "space", None),
        check_vma=False,
    )
```

time: 122 us -> 98.3 us (0.81)
  local copies, waits for them, and re-layouts: 22 us -> 5.28 us
  Pallas kernels: 100 us -> 92.7 us
    unnamed x7 -> x0, local copies, waits for them, and re-layouts: 12.6 us -> none
    pallas_call x2 -> x1, Pallas kernels: 23.8 us -> 16.3 us  [local(): pl.pallas_call(read_kernel, grid=(-(-columns // gw),), out_shape=jax.Shap...]
    broadcast_in_dim x1 -> x0, local copies, waits for them, and re-layouts: 5.37 us -> none  [local(): return out[None]]
    reshape x1, local copies, waits for them, and re-layouts: 1.46 us -> 2.7 us  [local(): gain.reshape(HEADS, dim, 1)]
where the time goes in v2:
time: 98.3 us; the launch traced here: 98 us
  Pallas kernels  92.7 us (94%)
  local copies, waits for them, and re-layouts  5.28 us (5%)
    pallas_call x1, Pallas kernels, local(): pl.pallas_call(functools.partial(exchange_kernel, n, space), out_shape=(j...  76.4 us
    pallas_call x1, Pallas kernels, local(): pl.pallas_call(read_kernel, grid=(-(-columns // gw),), out_shape=jax.Shap...  16.3 us
    reshape x1, local copies, waits for them, and re-layouts, local(): gain.reshape(HEADS, dim, 1)  2.7 us

profile of v2, /device:TPU:0, one launch (start us, length us, event | category | flops | bytes accessed | tf_op | source)
XLA Modules:
  0.0 98.0 jit_solution(13664713865291641440)
XLA Ops:
  0.0 2.7 %reshape.28.gain_ref = f32[20,112,1]{2,1,0:T(8,128)} reshape(f32[2240]{0:T(1024)} %param.8) | data formatting | bytes 17920 | tf_op jit(solution)/shard_map/reshape | solution.py:286
  2.7 1.4 %pad.4 = bf16[280,2304]{1,0:T(8,128)(2,1)S(1)} pad(bf16[280,2240]{1,0:T(8,128)(2,1)} %param.9, bf16[]{:T(256)} %constant.2.clone.1), padding=0_0x0_64 | pad | bytes 2544642 | tf_op jit(solution)/shard_map/jit(_pad)/pad | solution.py:226
  4.1 1.2 %copy.10 = bf16[35,6,8,384]{3,2,0,1:T(8,128)(2,1)} copy(bf16[35,6,8,384]{3,2,1,0:T(8,128)(2,1)S(1)} %bitcast.29) | data formatting | bytes 2580480 | tf_op jit(solution)/shard_map/reshape | solution.py:227
  5.3 76.4 %exchange.1 = (bf16[4,5,128,112]{3,2,1,0:T(8,128)(2,1)}, bf16[6,8,280,384]{3,2,1,0:T(8,128)(2,1)}) custom-call(bf16[20,112,640]{2,1,0:T(8,128)(2,1)} %bitcast.30, bf16[20,112,640]{2,1,0:T(8,128)(2,1)} %bitcast.31, bf16[6,280,384]{2,1,0:T(8,128)(2,1)} %bitcast.28), custom_call_target="tpu_custom_call" | custom-call | tf_op jit(solution)/shard_map/exchange/pallas_call | solution.py:235
  81.7 16.3 %read_project.1 = bf16[2240,640]{1,0:T(8,128)(2,1)} custom-call(bf16[20,112,640]{2,1,0:T(8,128)(2,1)} %bitcast.32, bf16[20,128,112]{2,1,0:T(8,128)(2,1)} %bitcast.33, f32[20,112,1]{2,1,0:T(8,128)} %reshape.28.gain_ref, bf16[6,2240,384]{2,1,0:T(8,128)(2,1)} %bitcast.27), custom_call_target="tpu_custom_call" | custom-call | tf_op jit(solution)/shard_map/read_project/pallas_call | solution.py:266

commit v3 on v2

--- a/solution.py
+++ b/solution.py
@@ -9,12 +9,15 @@
 
 HEADS = 20
 LANES = 128
+EARLY = (9, 14)
+BEFORE_SUM = 1
+PER_HOP = 1
 MESH = pl.DeviceIdType.MESH
 
 
 def exchange_kernel(
-    n, space, k_ref, v_ref, w_ref, state_ref, wg_ref,
-    keys, vals, ones, part_ref, landed, totals, arrived,
+    n, space, k_ref, v_ref, q_ref, w_ref, gain_ref, normed_ref, wg_ref,
+    keys, vals, asks, mixed, ones, state_ref, part_ref, landed, totals, arrived,
     local_sem, load_sem, rs_send, rs_recv, scan_send, scan_recv, ag_send, ag_recv,
     tm_send, tm_recv, y_send, y_recv, core_send, core_recv,
 ):
@@ -42,6 +45,7 @@
     loads = [
         pltpu.make_async_copy(k_ref, keys, load_sem.at[0]),
         pltpu.make_async_copy(v_ref, vals, load_sem.at[1]),
+        pltpu.make_async_copy(q_ref, asks, load_sem.at[2]),
     ]
     for load in loads:
         load.start()
@@ -96,28 +100,6 @@
             go(weight_hop(i, 0, d))
     own = pltpu.make_async_copy(w_ref, wg_ref.at[:, t], local_sem)
     own.start()
-
-    heads, dim, _ = keys.shape
-    ones[...] = jnp.ones_like(ones)
-    for load in loads:
-        load.wait()
-    share = part_ref.shape[1]
-
-    def one_state(h):
-        v = jnp.concatenate([vals[h], ones[...]], axis=0)
-        fk = jnp.maximum(keys[h], 0)
-        return lax.dot_general(
-            v, fk, (((1,), (1,)), ((), ())), preferred_element_type=jnp.float32
-        ).astype(part_ref.dtype)
-
-    for h in range(space * share):
-        part_ref[h // share, h % share] = (
-            one_state(h) if h < heads else jnp.zeros(part_ref.shape[2:], part_ref.dtype)
-        )
-
-    for r in range(1, space):
-        go(remote(part_ref.at[lax.rem(s + r, space)], landed.at[r],
-                  rs_send.at[r], rs_recv.at[r], peer(r)))
 
     pending = []
 
@@ -147,6 +129,32 @@
         if order:
             pass_on(order.pop(0))
 
+    heads, dim, _ = keys.shape
+    ones[...] = jnp.ones_like(ones)
+    for load in loads[:2]:
+        load.wait()
+    share = part_ref.shape[1]
+
+    def one_state(h):
+        v = jnp.concatenate([vals[h], ones[...]], axis=0)
+        fk = jnp.maximum(keys[h], 0)
+        return lax.dot_general(
+            v, fk, (((1,), (1,)), ((), ())), preferred_element_type=jnp.float32
+        ).astype(part_ref.dtype)
+
+    for h in range(space * share):
+        part_ref[h // share, h % share] = (
+            one_state(h) if h < heads else jnp.zeros(part_ref.shape[2:], part_ref.dtype)
+        )
+        if h in EARLY:
+            next_weight()
+
+    for r in range(1, space):
+        go(remote(part_ref.at[lax.rem(s + r, space)], landed.at[r],
+                  rs_send.at[r], rs_recv.at[r], peer(r)))
+
+    for _ in range(BEFORE_SUM):
+        next_weight()
     total = part_ref[s].astype(jnp.float32)
     for r in range(1, space):
         remote(part_ref.at[0], landed.at[r], rs_send.at[r], rs_recv.at[r], peer(r)).wait_recv()
@@ -156,7 +164,8 @@
         totals[k] = total.astype(totals.dtype)
         hop = remote(totals.at[k], arrived.at[k], scan_send.at[k], scan_recv.at[k], (flip(d), s))
         go(hop)
-        next_weight()
+        for _ in range(PER_HOP):
+            next_weight()
         hop.wait_recv()
         got = arrived[k].astype(jnp.float32)
         prefix = prefix + got * ((t // d) % 2).astype(jnp.float32)
@@ -168,11 +177,28 @@
         next_weight()
         if len(pending) > 1:
             settle(pending.pop(0))
+    for r in range(1, space):
+        slot = state_ref.at[lax.rem(s + space - r, space)]
+        remote(slot, slot, ag_send.at[r], ag_recv.at[r], peer(r)).wait_recv()
+    loads[2].wait()
+    rows = asks.shape[2]
+    squares = jnp.zeros((1, rows), jnp.float32)
+    for h in range(heads):
+        both = jnp.dot(
+            state_ref[h // share, h % share],
+            jnp.maximum(asks[h], 0),
+            preferred_element_type=jnp.float32,
+        )
+        tile = both[:dim] / (both[dim : dim + 1] + 1.0)
+        mixed[h] = tile
+        squares = squares + jnp.sum(tile * tile, axis=0, keepdims=True)
     while pending:
         settle(pending.pop(0))
-    for r in range(1, space):
-        slot = state_ref.at[lax.rem(s + space - r, space)]
-        remote(slot, slot, ag_send.at[r], ag_recv.at[r], peer(r)).wait_recv()
+    scale = lax.rsqrt(squares / (heads * dim) + 1e-06)
+    gain = jnp.broadcast_to(gain_ref[...], (8, heads * dim)).T
+    for h in range(heads):
+        mixed[h] = mixed[h] * scale * gain[h * dim : (h + 1) * dim, :1]
+    normed_ref[...] = mixed[...].reshape(heads * dim, rows).astype(normed_ref.dtype).T
     other = 1 - c
     for m in range(1, n):
         sources = [y * cores + other, space + other]
@@ -186,27 +212,13 @@
         copy.wait_send()
 
 
-def read_kernel(q_ref, state_ref, gain_ref, w_ref, out_ref, mixed, normed):
-    heads, dim, rows = q_ref.shape
-
-    @pl.when(pl.program_id(0) == 0)
-    def _():
-        squares = jnp.zeros((1, rows), jnp.float32)
-        for h in range(heads):
-            both = jnp.dot(
-                state_ref[h], jnp.maximum(q_ref[h], 0), preferred_element_type=jnp.float32
-            )
-            tile = both[:dim] / (both[dim : dim + 1] + 1.0)
-            mixed[h] = tile
-            squares = squares + jnp.sum(tile * tile, axis=0, keepdims=True)
-        scale = lax.rsqrt(squares / (heads * dim) + 1e-06)
-        for h in range(heads):
-            mixed[h] = mixed[h] * scale * gain_ref[h]
-        flat = mixed[...].reshape(heads * dim, rows).astype(normed.dtype)
-        normed[...] = flat.T
-
+def project_kernel(normed_ref, w_ref, out_ref):
     out_ref[...] = (
-        jnp.dot(normed[...], w_ref[0], preferred_element_type=jnp.float32)
+        jnp.dot(
+            normed_ref[...],
+            jnp.concatenate([w_ref[0], w_ref[1]], axis=1),
+            preferred_element_type=jnp.float32,
+        )
         .astype(out_ref.dtype)
         .T
     )
@@ -232,24 +244,27 @@
     steps = n.bit_length() - 1
     dma = pltpu.SemaphoreType.DMA
     piece = (share, dim + extra, dim)
-    prefix, wg = pl.pallas_call(
+    normed, wg = pl.pallas_call(
         functools.partial(exchange_kernel, n, space),
         out_shape=(
-            jax.ShapeDtypeStruct((space,) + piece, jnp.bfloat16),
+            jax.ShapeDtypeStruct((rows, width), jnp.bfloat16),
             jax.ShapeDtypeStruct((groups, n, shard, gw), jnp.bfloat16),
         ),
-        in_specs=[pl.BlockSpec(memory_space=pl.ANY)] * 3,
+        in_specs=[pl.BlockSpec(memory_space=pl.ANY)] * 4 + [vmem],
         out_specs=(vmem, pl.BlockSpec(memory_space=pl.ANY)),
         scratch_shapes=[
             pltpu.VMEM((HEADS, dim, rows), jnp.bfloat16),
             pltpu.VMEM((HEADS, dim, rows), jnp.bfloat16),
+            pltpu.VMEM((HEADS, dim, rows), jnp.bfloat16),
+            pltpu.VMEM((HEADS, dim, rows), jnp.float32),
             pltpu.VMEM((extra, rows), jnp.bfloat16),
+            pltpu.VMEM((space,) + piece, jnp.bfloat16),
             pltpu.VMEM((space,) + piece, jnp.bfloat16),
             pltpu.VMEM((space,) + piece, jnp.bfloat16),
             pltpu.VMEM((steps,) + piece, jnp.bfloat16),
             pltpu.VMEM((steps,) + piece, jnp.bfloat16),
             dma,
-            dma((2,)),
+            dma((3,)),
             dma((space,)), dma((space,)),
             dma((steps,)), dma((steps,)),
             dma((space,)), dma((space,)),
@@ -261,31 +276,20 @@
             collective_id=0, has_side_effects=True, vmem_limit_bytes=56 * 1024 * 1024
         ),
         name="exchange",
-    )(by_head(keys), by_head(values), w)
+    )(by_head(keys), by_head(values), by_head(queries), w, gain.reshape(1, width))
 
     out = pl.pallas_call(
-        read_kernel,
-        grid=(-(-columns // gw),),
+        project_kernel,
+        grid=(-(-columns // (2 * gw)),),
         out_shape=jax.ShapeDtypeStruct((columns, rows), jnp.bfloat16),
         in_specs=[
-            pl.BlockSpec((HEADS, dim, rows), lambda i: (0, 0, 0)),
-            pl.BlockSpec((space * share, dim + extra, dim), lambda i: (0, 0, 0)),
-            pl.BlockSpec((HEADS, dim, 1), lambda i: (0, 0, 0)),
-            pl.BlockSpec((1, n * shard, gw), lambda i: (i, 0, 0)),
+            pl.BlockSpec((rows, width), lambda i: (0, 0)),
+            pl.BlockSpec((2, n * shard, gw), lambda i: (i, 0, 0)),
         ],
-        out_specs=pl.BlockSpec((gw, rows), lambda i: (i, 0)),
-        scratch_shapes=[
-            pltpu.VMEM((HEADS, dim, rows), jnp.float32),
-            pltpu.VMEM((rows, width), jnp.bfloat16),
-        ],
+        out_specs=pl.BlockSpec((2 * gw, rows), lambda i: (i, 0)),
         compiler_params=big,
-        name="read_project",
-    )(
-        by_head(queries),
-        prefix.reshape((space * share,) + piece[1:]),
-        gain.reshape(HEADS, dim, 1),
-        wg.reshape(groups, n * shard, gw),
-    )
+        name="project",
+    )(normed, wg.reshape(groups, n * shard, gw))
     return out.T[None]
 
 

time: 98.3 us -> 93.7 us (0.953)
  Pallas kernels: 92.7 us -> 89.5 us
  local copies, waits for them, and re-layouts: 5.28 us -> 3.89 us
    pallas_call x1, Pallas kernels: 16.3 us -> 11.4 us  [local(): pl.pallas_call(project_kernel, grid=(-(-columns // (2 * gw)),), out_shape...]
    pallas_call x1, Pallas kernels: 76.4 us -> 78.1 us  [local(): pl.pallas_call(functools.partial(exchange_kernel, n, space), out_shape=(j...]
    reshape x1, local copies, waits for them, and re-layouts: 2.7 us -> 1.31 us  [local(): gain.reshape(1, width)]
where the time goes in v3:
time: 93.7 us; the launch traced here: 93.4 us
  Pallas kernels  89.5 us (96%)
  local copies, waits for them, and re-layouts  3.89 us (4%)
    pallas_call x1, Pallas kernels, local(): pl.pallas_call(functools.partial(exchange_kernel, n, space), out_shape=(j...  78.1 us
    pallas_call x1, Pallas kernels, local(): pl.pallas_call(project_kernel, grid=(-(-columns // (2 * gw)),), out_shape...  11.4 us

profile of v3, /device:TPU:0, one launch (start us, length us, event | category | flops | bytes accessed | tf_op | source)
XLA Modules:
  0.0 93.4 jit_solution(2166813192520853767)
XLA Ops:
  0.0 1.3 %reshape.22.gain_ref = f32[1,2240]{1,0:T(1,128)} reshape(f32[2240]{0:T(1024)} %param.8) | data formatting | bytes 17920 | tf_op jit(solution)/shard_map/reshape | solution.py:279
  1.3 1.4 %pad.4 = bf16[280,2304]{1,0:T(8,128)(2,1)S(1)} pad(bf16[280,2240]{1,0:T(8,128)(2,1)} %param.9, bf16[]{:T(256)} %constant.2.clone.1), padding=0_0x0_64 | pad | bytes 2544642 | tf_op jit(solution)/shard_map/jit(_pad)/pad | solution.py:238
  2.7 1.2 %copy.9 = bf16[35,6,8,384]{3,2,0,1:T(8,128)(2,1)} copy(bf16[35,6,8,384]{3,2,1,0:T(8,128)(2,1)S(1)} %bitcast.28) | data formatting | bytes 2580480 | tf_op jit(solution)/shard_map/reshape | solution.py:239
  3.9 78.1 %exchange.1 = (bf16[640,2240]{1,0:T(8,128)(2,1)}, bf16[6,8,280,384]{3,2,1,0:T(8,128)(2,1)}) custom-call(bf16[20,112,640]{2,1,0:T(8,128)(2,1)} %bitcast.29, bf16[20,112,640]{2,1,0:T(8,128)(2,1)} %bitcast.30, bf16[20,112,640]{2,1,0:T(8,128)(2,1)} %bitcast.31, bf16[6,280,384]{2,1,0:T(8,128)(2,1)} %bitcast.27, f32[1,2240]{1,0:T(1,128)} %reshape.22.gain_ref), custom_call_target="tpu_custom_call" | custom-call | tf_op jit(solution)/shard_map/exchange/pallas_call | solution.py:247
  82.0 11.4 %project.1 = bf16[2240,640]{1,0:T(8,128)(2,1)} custom-call(bf16[640,2240]{1,0:T(8,128)(2,1)} %get-tuple-element.7.normed_ref, bf16[6,2240,384]{2,1,0:T(8,128)(2,1)} %bitcast.26), custom_call_target="tpu_custom_call" | custom-call | tf_op jit(solution)/shard_map/project/pallas_call | solution.py:281
